TPU v7x, 128 devices: a whole 4x4x4 slice. The times are simulated.
128 devices in a mesh: oi: 8 (over y, z_hi), oj: 16 (over z_lo, x, core).
Axes of the slice: x: 4, y: 4, z: 4 (z_hi: 2, z_lo: 2; z = z_hi * 2 + z_lo), core: 2. Of those that a mesh axis runs over, the one named last changes fastest.
Arguments:
- b_tensor: bfloat16 [128, 1536, 512], P(('oi', 'oj')), may hold values from -2.5 to 2.5
- occ_energy: bfloat16 [128], P(('oi', 'oj')), may hold values from -2 to -0.29882812
- dom_blocks: int32 [128, 4], P(('oi', 'oj')), may hold values from 0 to 63
- pair_cols: int32 [128, 7], P(('oi', 'oj')), may hold values from 0 to 15, as said below
- pao_energy: float32 [64, 128], replicated, may hold values from 0.5 to 3
Outputs:
- gamma_tiles: bfloat16 [128, 1536, 512], P(('oi', 'oj'))
- aux_density: bfloat16 [1536, 1536], P(('oi', 'oj'))
Inputs may be any that keep to these rules, and one draw needn't show every extreme that they name: `pair_cols`: each row names 7 different positions, never the orbital's own position o mod 16.
All inputs are finite; a program needn't handle non-finite values.
Results may differ from a plain program's by a relative error of at most 0.0031.
Values may be sent and summed in bfloat16 or wider, within the bound.
A program may use at most 128 MiB of HBM per device.

v0:
```python
import jax
import jax.numpy as jnp
from jax import lax
from jax.sharding import PartitionSpec as P


def body(b_tensor, occ_energy, dom_blocks, pair_cols, pao_energy):
    row_b, row_occ, row_dom, row_pairs = (
        lax.all_gather(b_tensor, "oj", axis=0, tiled=True),
        lax.all_gather(occ_energy, "oj", axis=0, tiled=True),
        lax.all_gather(dom_blocks, "oj", axis=0, tiled=True),
        lax.all_gather(pair_cols, "oj", axis=0, tiled=True),
    )
    row_width = lax.axis_size("oj")
    position = lax.axis_index("oj")
    domain_size = b_tensor.shape[2]
    virtual = pao_energy[row_dom].reshape(row_width, domain_size)
    occupied = row_occ.astype(jnp.float32)
    own_block = b_tensor[0]
    gamma_tile = jnp.zeros((b_tensor.shape[1], domain_size), jnp.float32)
    outgoing = jnp.zeros((row_width, domain_size, domain_size), jnp.bfloat16)
    for pair_slot in range(pair_cols.shape[1]):
        partner = row_pairs[position, pair_slot]
        partner_block = lax.dynamic_index_in_dim(row_b, partner, 0, keepdims=False)
        intersection = lax.dot_general(
            own_block, partner_block, (((0,), (0,)), ((), ())), preferred_element_type=jnp.float32
        )
        denominator = (
            virtual[position][:, None]
            + virtual[partner][None, :]
            - occupied[position]
            - occupied[partner]
        )
        tile = (-intersection / denominator).astype(jnp.bfloat16)
        gamma_tile = gamma_tile + lax.dot_general(
            partner_block, tile, (((1,), (1,)), ((), ())), preferred_element_type=jnp.float32
        )
        outgoing = lax.dynamic_update_index_in_dim(outgoing, tile, partner, 0)
    incoming = jnp.any(row_pairs == position, axis=1).astype(jnp.int32)
    sources = jnp.argsort(1 - incoming, stable=True)
    incoming_total = jnp.sum(incoming)
    received = lax.all_to_all(outgoing, "oj", split_axis=0, concat_axis=0, tiled=True)

    def add_incoming(step_index, total_sum):
        source = sources[step_index]
        source_block = lax.dynamic_index_in_dim(row_b, source, 0, keepdims=False)
        tile = lax.dynamic_index_in_dim(received, source, 0, keepdims=False)
        return total_sum + jnp.dot(source_block, tile, preferred_element_type=jnp.float32)

    gamma_tile = lax.fori_loop(0, incoming_total, add_incoming, gamma_tile)
    gamma_round = gamma_tile.astype(jnp.bfloat16)
    factor = 1.0 / (row_width * lax.axis_size("oi"))
    row_count = b_tensor.shape[1] // lax.axis_size(("oi", "oj"))
    piece = lax.slice_in_dim(gamma_round, 0, lax.axis_size(("oi", "oj")) * row_count, axis=0)
    density = lax.psum_scatter(
        factor
        * lax.dot_general(
            piece, own_block, (((1,), (1,)), ((), ())), preferred_element_type=jnp.float32
        ),
        ("oi", "oj"),
        scatter_dimension=0,
        tiled=True,
    )
    return (gamma_round[None], density.astype(jnp.bfloat16))


def solution(mesh):
    in_specs = (
        P(("oi", "oj"), None, None),
        P(("oi", "oj")),
        P(("oi", "oj"), None),
        P(("oi", "oj"), None),
        P(),
    )
    out_specs = (P(("oi", "oj"), None, None), P(("oi", "oj"), None))
    return jax.shard_map(body, mesh=mesh, in_specs=in_specs, out_specs=out_specs, check_vma=False)
```

profile of v0, /device:TPU:1, one launch (start us, length us, event | category | flops | bytes accessed | tf_op | source)
XLA Modules:
  0.0 886.7 jit_solution(18337964718711238479)
XLA Ops:
  10.6 28.9 %all-reduce = bf16[16]{0:T(256)(128)(2,1)S(1)} all-reduce(bf16[16]{0:T(256)(128)(2,1)S(1)} %dynamic-update-slice), channel_id=1, replica_groups=mesh['oi'=8,'oj'=16] {'oj'}, use_global_device_ids=true, to_apply=%add | all-reduce | flops 16 | bytes 64
  39.5 19.8 %all-gather = s32[16,1,7]{2,1,0:T(1,128)S(1)} all-gather(s32[1,1,7]{2,1,0:T(1,128)} %bitcast.242), channel_id=1, replica_groups=mesh['oi'=8,'oj'=16] {'oj'}, dimensions={0}, use_global_device_ids=true | all-gather | bytes 476 | tf_op jit(solution)/shard_map/all_gather | solution.py:12
  68.8 17.9 %all-gather.1 = s32[16,1,4]{2,1,0:T(1,128)S(1)} all-gather(s32[1,1,4]{2,1,0:T(1,128)} %bitcast.243), channel_id=1, replica_groups=mesh['oi'=8,'oj'=16] {'oj'}, dimensions={0}, use_global_device_ids=true | all-gather | bytes 272 | tf_op jit(solution)/shard_map/all_gather | solution.py:11
  92.8 52.1 %all-gather.4.cloned.1.call-done = bf16[16,1536,512]{2,1,0:T(8,128)(2,1)} async-done(((bf16[1,1536,512]{2,1,0:T(8,128)(2,1)}), bf16[16,1536,512]{2,1,0:T(8,128)(2,1)}) %all-gather.4.cloned.1.call-update) | async-done | bytes 25165840 | tf_op jit(solution)/shard_map/all_gather | solution.py:9
  144.9 4.3 divide_convert_fusion.6
  150.2 3.6 divide_convert_fusion.5
  154.8 3.7 divide_convert_fusion.4
  159.6 3.6 divide_convert_fusion.3
  164.2 4.5 divide_convert_fusion.2
  170.7 4.4 divide_convert_fusion.1
  177.2 4.5 divide_convert_fusion
  183.0 4.1 broadcast_in_dim.32
  193.0 5.1 all-to-all-start
  217.5 93.1 %all-to-all-done = bf16[16,512,512]{2,1,0:T(8,128)(2,1)} async-done(((bf16[16,512,512]{2,1,0:T(8,128)(2,1)}), bf16[16,512,512]{2,1,0:T(8,128)(2,1)}, u32[]{:S(2)}, u32[]{:S(2)}) %all-to-all-start) | async-done | bytes 8388640 | tf_op jit(solution)/shard_map/all_to_all | solution.py:42
  310.6 87.2 %while.10 = (s32[]{:T(128)}, f32[1536,512]{1,0:T(8,128)S(1)}, s32[]{:T(128)}, s32[16]{0:T(128)S(1)}, bf16[16,1536,512]{2,1,0:T(8,128)(2,1)}, /*index=5*/bf16[16,...) while((s32[]{:T(128)}, f32[1536,512]{1,0:T(8,128)S(1)}, s32[]{:T(128)}, s32[16]{0:T(128)S(1)}, ...), condition=%wide.region_4.5_spmd, body=%wide.region_3.4_spmd.sunk | while | flops 806092800 | bytes 8389805 | solution.py:50
  397.8 6.5 convolution_multiply_fusion
  404.3 350.8 %fusion = f32[16,1536]{1,0:T(8,128)S(1)} fusion(f32[1536,1536]{1,0:T(8,128)} %convolution_multiply_fusion), kind=kCustom, calls=%all-reduce-scatter | all-reduce-scatter fusion | flops 3145729 | bytes 9535488
  755.0 3.7 collective-permute-start
  768.1 12.1 %collective-permute-start.15 = (bf16[16,1536]{1,0:T(8,128)(2,1)S(1)}, bf16[16,1536]{1,0:T(8,128)(2,1)S(1)}, u32[]{:S(2)}, u32[]{:S(2)}) collective-permute-start(bf16[16,1536]{1,0:T(8,128)(2,1)S(1)} %convert.66), channel_id=1, source_target_pairs={{0,16},{1,17},{2,18},{3,19},{4,20},{5,21},{6,22},{7,23},{8,24},{9,... | collective-permute-start | bytes 147464
  783.3 12.8 %collective-permute-start.17 = (bf16[16,1536]{1,0:T(8,128)(2,1)S(1)}, bf16[16,1536]{1,0:T(8,128)(2,1)S(1)}, u32[]{:S(2)}, u32[]{:S(2)}) collective-permute-start(bf16[16,1536]{1,0:T(8,128)(2,1)S(1)} %convert.66), channel_id=1, source_target_pairs={{0,18},{1,19},{2,20},{3,21},{4,22},{5,23},{6,24},{7,25},{8,26},{9,... | collective-permute-start | bytes 147464
  796.2 5.5 collective-permute-start.18
  820.7 4.0 collective-permute-start.27
  832.5 4.2 collective-permute-start.4
  852.5 26.7 %concatenate = bf16[524,1536]{1,0:T(8,128)(2,1)S(1)} concatenate(bf16[12,1536]{1,0:T(8,128)(2,1)S(1)} %collective-permute-done.31, bf16[16,1536]{1,0:T(8,128)(2,1)} %collective-permute-done.30, bf16[16,1536]{1,0:T(8,128)(2,1)} %collective-permute-done.29, bf16[16,1536]{1,0:T(8,128)(2,1)} %collective-permute-done.28, bf16[16,1536]{1,0:T(8,128)(2,1)} %copy-done.31, ...), dimensions={0} | concatenate | bytes 3268608
  (204 shorter events, 142.4 us)
Async XLA Ops:
  7.2 137.7 %all-gather.4.cloned.1.call-start = ((), (), s32[]{:S(2)}) async-start(), calls=%async_computation.1 | async-start | bytes 26738688 | tf_op jit(solution)/shard_map/all_gather | solution.py:9
  193.0 117.6 %all-to-all-start = ((bf16[16,512,512]{2,1,0:T(8,128)(2,1)}), bf16[16,512,512]{2,1,0:T(8,128)(2,1)}, u32[]{:S(2)}, u32[]{:S(2)}) async-start(bf16[16,512,512]{2,1,0:T(8,128)(2,1)} %constant_dynamic-update-slice_fusion), calls=%async_computation | async-start | bytes 16777216 | tf_op jit(solution)/shard_map/all_to_all | solution.py:42
  755.0 10.5 %collective-permute-start = (bf16[16,1536]{1,0:T(8,128)(2,1)S(1)}, bf16[16,1536]{1,0:T(8,128)(2,1)S(1)}, u32[]{:S(2)}, u32[]{:S(2)}) collective-permute-start(bf16[16,1536]{1,0:T(8,128)(2,1)S(1)} %convert.66), channel_id=1, source_target_pairs={{0,1},{1,2},{2,3},{3,4},{4,5},{5,6},{6,7},{7,8},{8,9},{9,10},{10,1... | collective-permute-start | bytes 147464
  762.7 17.5 %collective-permute-start.11 = (bf16[16,1536]{1,0:T(8,128)(2,1)S(1)}, bf16[16,1536]{1,0:T(8,128)(2,1)S(1)}, u32[]{:S(2)}, u32[]{:S(2)}) collective-permute-start(bf16[16,1536]{1,0:T(8,128)(2,1)S(1)} %convert.66), channel_id=1, source_target_pairs={{0,12},{1,13},{2,14},{3,15},{4,16},{5,17},{6,18},{7,19},{8,20},{9,... | collective-permute-start | bytes 147464
  764.0 19.3 %collective-permute-start.12 = (bf16[16,1536]{1,0:T(8,128)(2,1)S(1)}, bf16[16,1536]{1,0:T(8,128)(2,1)S(1)}, u32[]{:S(2)}, u32[]{:S(2)}) collective-permute-start(bf16[16,1536]{1,0:T(8,128)(2,1)S(1)} %convert.66), channel_id=1, source_target_pairs={{0,13},{1,14},{2,15},{3,16},{4,17},{5,18},{6,19},{7,20},{8,21},{9,... | collective-permute-start | bytes 147464
  765.5 30.6 %collective-permute-start.13 = (bf16[16,1536]{1,0:T(8,128)(2,1)S(1)}, bf16[16,1536]{1,0:T(8,128)(2,1)S(1)}, u32[]{:S(2)}, u32[]{:S(2)}) collective-permute-start(bf16[16,1536]{1,0:T(8,128)(2,1)S(1)} %convert.66), channel_id=1, source_target_pairs={{0,14},{1,15},{2,16},{3,17},{4,18},{5,19},{6,20},{7,21},{8,22},{9,... | collective-permute-start | bytes 147464
  766.8 34.8 %collective-permute-start.14 = (bf16[16,1536]{1,0:T(8,128)(2,1)S(1)}, bf16[16,1536]{1,0:T(8,128)(2,1)S(1)}, u32[]{:S(2)}, u32[]{:S(2)}) collective-permute-start(bf16[16,1536]{1,0:T(8,128)(2,1)S(1)} %convert.66), channel_id=1, source_target_pairs={{0,15},{1,16},{2,17},{3,18},{4,19},{5,20},{6,21},{7,22},{8,23},{9,... | collective-permute-start | bytes 147464
  768.1 37.0 %collective-permute-start.15 = (bf16[16,1536]{1,0:T(8,128)(2,1)S(1)}, bf16[16,1536]{1,0:T(8,128)(2,1)S(1)}, u32[]{:S(2)}, u32[]{:S(2)}) collective-permute-start(bf16[16,1536]{1,0:T(8,128)(2,1)S(1)} %convert.66), channel_id=1, source_target_pairs={{0,16},{1,17},{2,18},{3,19},{4,20},{5,21},{6,22},{7,23},{8,24},{9,... | collective-permute-start | bytes 147464
  780.2 28.0 %collective-permute-start.16 = (bf16[16,1536]{1,0:T(8,128)(2,1)S(1)}, bf16[16,1536]{1,0:T(8,128)(2,1)S(1)}, u32[]{:S(2)}, u32[]{:S(2)}) collective-permute-start(bf16[16,1536]{1,0:T(8,128)(2,1)S(1)} %convert.66), channel_id=1, source_target_pairs={{0,17},{1,18},{2,19},{3,20},{4,21},{5,22},{6,23},{7,24},{8,25},{9,... | collective-permute-start | bytes 147464
  783.3 26.9 %collective-permute-start.17 = (bf16[16,1536]{1,0:T(8,128)(2,1)S(1)}, bf16[16,1536]{1,0:T(8,128)(2,1)S(1)}, u32[]{:S(2)}, u32[]{:S(2)}) collective-permute-start(bf16[16,1536]{1,0:T(8,128)(2,1)S(1)} %convert.66), channel_id=1, source_target_pairs={{0,18},{1,19},{2,20},{3,21},{4,22},{5,23},{6,24},{7,25},{8,26},{9,... | collective-permute-start | bytes 147464
  796.2 16.0 %collective-permute-start.18 = (bf16[16,1536]{1,0:T(8,128)(2,1)S(1)}, bf16[16,1536]{1,0:T(8,128)(2,1)S(1)}, u32[]{:S(2)}, u32[]{:S(2)}) collective-permute-start(bf16[16,1536]{1,0:T(8,128)(2,1)S(1)} %convert.66), channel_id=1, source_target_pairs={{0,19},{1,20},{2,21},{3,22},{4,23},{5,24},{6,25},{7,26},{8,27},{9,... | collective-permute-start | bytes 147464
  801.7 11.9 %collective-permute-start.19 = (bf16[16,1536]{1,0:T(8,128)(2,1)S(1)}, bf16[16,1536]{1,0:T(8,128)(2,1)S(1)}, u32[]{:S(2)}, u32[]{:S(2)}) collective-permute-start(bf16[16,1536]{1,0:T(8,128)(2,1)S(1)} %convert.66), channel_id=1, source_target_pairs={{0,20},{1,21},{2,22},{3,23},{4,24},{5,25},{6,26},{7,27},{8,28},{9,... | collective-permute-start | bytes 147464
  813.5 11.2 %collective-permute-start.23 = (bf16[16,1536]{1,0:T(8,128)(2,1)S(1)}, bf16[16,1536]{1,0:T(8,128)(2,1)S(1)}, u32[]{:S(2)}, u32[]{:S(2)}) collective-permute-start(bf16[16,1536]{1,0:T(8,128)(2,1)S(1)} %convert.66), channel_id=1, source_target_pairs={{0,24},{1,25},{2,26},{3,27},{4,28},{5,29},{6,30},{7,31},{8,32},{9,... | collective-permute-start | bytes 147464
  815.5 11.3 %collective-permute-start.24 = (bf16[16,1536]{1,0:T(8,128)(2,1)S(1)}, bf16[16,1536]{1,0:T(8,128)(2,1)S(1)}, u32[]{:S(2)}, u32[]{:S(2)}) collective-permute-start(bf16[16,1536]{1,0:T(8,128)(2,1)S(1)} %convert.66), channel_id=1, source_target_pairs={{0,25},{1,26},{2,27},{3,28},{4,29},{5,30},{6,31},{7,32},{8,33},{9,... | collective-permute-start | bytes 147464
  818.0 10.6 %collective-permute-start.25 = (bf16[16,1536]{1,0:T(8,128)(2,1)S(1)}, bf16[16,1536]{1,0:T(8,128)(2,1)S(1)}, u32[]{:S(2)}, u32[]{:S(2)}) collective-permute-start(bf16[16,1536]{1,0:T(8,128)(2,1)S(1)} %convert.66), channel_id=1, source_target_pairs={{0,26},{1,27},{2,28},{3,29},{4,30},{5,31},{6,32},{7,33},{8,34},{9,... | collective-permute-start | bytes 147464
  819.3 11.2 %collective-permute-start.26 = (bf16[16,1536]{1,0:T(8,128)(2,1)S(1)}, bf16[16,1536]{1,0:T(8,128)(2,1)S(1)}, u32[]{:S(2)}, u32[]{:S(2)}) collective-permute-start(bf16[16,1536]{1,0:T(8,128)(2,1)S(1)} %convert.66), channel_id=1, source_target_pairs={{0,27},{1,28},{2,29},{3,30},{4,31},{5,32},{6,33},{7,34},{8,35},{9,... | collective-permute-start | bytes 147464
  820.7 11.7 %collective-permute-start.27 = (bf16[16,1536]{1,0:T(8,128)(2,1)S(1)}, bf16[16,1536]{1,0:T(8,128)(2,1)S(1)}, u32[]{:S(2)}, u32[]{:S(2)}) collective-permute-start(bf16[16,1536]{1,0:T(8,128)(2,1)S(1)} %convert.66), channel_id=1, source_target_pairs={{0,28},{1,29},{2,30},{3,31},{4,32},{5,33},{6,34},{7,35},{8,36},{9,... | collective-permute-start | bytes 147464
  824.8 12.1 %collective-permute-start.28 = (bf16[16,1536]{1,0:T(8,128)(2,1)S(1)}, bf16[16,1536]{1,0:T(8,128)(2,1)}, u32[]{:S(2)}, u32[]{:S(2)}) collective-permute-start(bf16[16,1536]{1,0:T(8,128)(2,1)S(1)} %convert.66), channel_id=1, source_target_pairs={{0,29},{1,30},{2,31},{3,32},{4,33},{5,34},{6,35},{7,36},{8,37},{9,... | collective-permute-start | bytes 147464
  826.8 12.6 %collective-permute-start.29 = (bf16[16,1536]{1,0:T(8,128)(2,1)S(1)}, bf16[16,1536]{1,0:T(8,128)(2,1)}, u32[]{:S(2)}, u32[]{:S(2)}) collective-permute-start(bf16[16,1536]{1,0:T(8,128)(2,1)S(1)} %convert.66), channel_id=1, source_target_pairs={{0,30},{1,31},{2,32},{3,33},{4,34},{5,35},{6,36},{7,37},{8,38},{9,... | collective-permute-start | bytes 147464
  828.7 12.3 %collective-permute-start.3 = (bf16[16,1536]{1,0:T(8,128)(2,1)S(1)}, bf16[16,1536]{1,0:T(8,128)(2,1)}, u32[]{:S(2)}, u32[]{:S(2)}) collective-permute-start(bf16[16,1536]{1,0:T(8,128)(2,1)S(1)} %convert.66), channel_id=1, source_target_pairs={{0,4},{1,5},{2,6},{3,7},{4,8},{5,9},{6,10},{7,11},{8,12},{9,13},{1... | collective-permute-start | bytes 147464
  830.6 13.1 %collective-permute-start.30 = (bf16[16,1536]{1,0:T(8,128)(2,1)S(1)}, bf16[16,1536]{1,0:T(8,128)(2,1)}, u32[]{:S(2)}, u32[]{:S(2)}) collective-permute-start(bf16[16,1536]{1,0:T(8,128)(2,1)S(1)} %convert.66), channel_id=1, source_target_pairs={{0,31},{1,32},{2,33},{3,34},{4,35},{5,36},{6,37},{7,38},{8,39},{9,... | collective-permute-start | bytes 147464
  832.5 14.3 %collective-permute-start.4 = (bf16[16,1536]{1,0:T(8,128)(2,1)S(1)}, bf16[16,1536]{1,0:T(8,128)(2,1)}, u32[]{:S(2)}, u32[]{:S(2)}) collective-permute-start(bf16[16,1536]{1,0:T(8,128)(2,1)S(1)} %convert.66), channel_id=1, source_target_pairs={{0,5},{1,6},{2,7},{3,8},{4,9},{5,10},{6,11},{7,12},{8,13},{9,14},{... | collective-permute-start | bytes 147464
  836.9 14.3 %collective-permute-start.5 = (bf16[16,1536]{1,0:T(8,128)(2,1)S(1)}, bf16[16,1536]{1,0:T(8,128)(2,1)S(1)}, u32[]{:S(2)}, u32[]{:S(2)}) collective-permute-start(bf16[16,1536]{1,0:T(8,128)(2,1)S(1)} %convert.66), channel_id=1, source_target_pairs={{0,6},{1,7},{2,8},{3,9},{4,10},{5,11},{6,12},{7,13},{8,14},{9,15},... | collective-permute-start | bytes 147464
  839.4 11.9 %collective-permute-start.6 = (bf16[16,1536]{1,0:T(8,128)(2,1)S(1)}, bf16[16,1536]{1,0:T(8,128)(2,1)S(1)}, u32[]{:S(2)}, u32[]{:S(2)}) collective-permute-start(bf16[16,1536]{1,0:T(8,128)(2,1)S(1)} %convert.66), channel_id=1, source_target_pairs={{0,7},{1,8},{2,9},{3,10},{4,11},{5,12},{6,13},{7,14},{8,15},{9,16}... | collective-permute-start | bytes 147464
  (46 other events, 681.7 us)
Sparse Core Ops, SparseCore 0:
  9.7 135.1 all-gather.3
where the time goes:
time: 894 us; the launch traced here: 887 us
  blocking collectives  417 us (47%)
  waiting for transfers between devices  146 us (16%)
  starting transfers between devices  99.1 us (11%)
  matrix products  90.9 us (10%)
  local copies, waits for them, and re-layouts  61.1 us (7%)
  loops' own time  39.5 us (4%)
  between operations  29 us (3%)
    unnamed x2, blocking collectives  380 us
    unnamed x32, starting transfers between devices  93.9 us
    all_to_all x1, waiting for transfers between devices, body(): lax.all_to_all(outgoing, 'oj', split_axis=0, concat_axis=0, tiled=True)  93.1 us
    all_gather x1, waiting for transfers between devices, body(): lax.all_gather(b_tensor, 'oj', axis=0, tiled=True)  52.1 us
    another operation x1, loops' own time, body(): gamma_tile = lax.fori_loop(0, incoming_total, add_incoming, gamma_tile)  39.5 us
    dot_general x15, matrix products, add_incoming(): jnp.dot(source_block, tile, preferred_element_type=jnp.float32)  38.9 us
    unnamed x77, local copies, waits for them, and re-layouts  30.1 us
    dot_general x7, matrix products, body(): lax.dot_general(own_block, partner_block, (((0,), (0,)), ((), ())), prefe...  28.6 us
  transfers between devices with their start and end apart: 34, of which 3 were waited for; matrix products, arithmetic and copies ran while one was open for 3% of the time, Pallas kernels for 0%

commit v1 on v0

v1 whole, which is shorter than its diff:
```python
import functools

import jax
import jax.numpy as jnp
from jax import lax
from jax.experimental import pallas as pl
from jax.experimental.pallas import tpu as pltpu
from jax.sharding import PartitionSpec as P

MESH = pl.DeviceIdType.MESH
PLUS, MINUS, ZED, SIBLING = range(4)
CHIPS_X, CHIPS_Z, CORES = 4, 2, 2
ROW = CHIPS_X * CHIPS_Z * CORES


def dot_nt(lhs, rhs):
    return lax.dot_general(lhs, rhs, (((1,), (1,)), ((), ())), preferred_element_type=jnp.float32)


def kernel(
    n_oi, b_hbm, occ_ref, dom_ref, pair_ref, pao_ref, gamma_out, dens_out,
    ball, bt, gsum, gout, gall, mcat, dacc, dpart, dall, small, vcol,
    link_send, piece_recv, small_send, small_recv, gam_send, gam_recv, den_send, den_recv, local_sem,
):
    naux, dom = b_hbm.shape[1], b_hbm.shape[2]
    blocks = dom // 128
    piece_rows = naux // 3
    slice_rows = naux // ROW
    strip = slice_rows // n_oi
    oi, oj = lax.axis_index("oi"), lax.axis_index("oj")
    core, x, z = lax.rem(oj, 2), lax.rem(oj // 2, CHIPS_X), oj // (CHIPS_X * CORES)

    def chip_at(dx, dz):
        return lax.rem(z + dz, CHIPS_Z) * CHIPS_X + lax.rem(x + dx, CHIPS_X)

    def place(dx, dz):
        return chip_at(dx, dz) * CORES + core

    sibling = oj + 1 - 2 * core
    link_to = {PLUS: place(1, 0), MINUS: place(3, 0), ZED: place(0, 1), SIBLING: sibling}
    first_owner = oj * n_oi
    my_slice = (oi * ROW + oj) // n_oi
    me = oi * ROW + oj
    self_owner = jnp.logical_and(first_owner <= me, me < first_owner + n_oi)

    def owner(t):
        flat = first_owner + t
        return flat // ROW, lax.rem(flat, ROW)

    barrier = pltpu.get_barrier_semaphore()
    for step in range(1, ROW):
        pl.semaphore_signal(barrier, inc=1, device_id=(oi, lax.rem(oj + step, ROW)), device_id_type=MESH)
    for t in range(n_oi):
        @pl.when(first_owner + t != me)
        def _():
            pl.semaphore_signal(barrier, inc=1, device_id=owner(t), device_id_type=MESH)

        @pl.when(jnp.logical_or(oi != t, oj != my_slice))
        def _():
            pl.semaphore_signal(barrier, inc=1, device_id=(t, my_slice), device_id_type=MESH)
    pl.semaphore_wait(barrier, ROW - 1 + 2 * n_oi - 2 * self_owner.astype(jnp.int32))

    counts = [0, 0, 0, 0]
    started = []

    def copy_of(slot, k, link, own=False):
        rows = pl.ds(k * piece_rows, piece_rows)
        copy = pltpu.make_async_remote_copy(
            src_ref=b_hbm.at[0, rows] if own else ball.at[slot, rows],
            dst_ref=ball.at[slot, rows],
            send_sem=link_send.at[link, counts[link]],
            recv_sem=piece_recv.at[slot, k],
            device_id=(oi, link_to[link]),
            device_id_type=MESH,
        )
        counts[link] += 1
        return copy

    def send(slot, k, link, own=False):
        copy = copy_of(slot, k, link, own)
        copy.start()
        started.append(copy)

    def wait_piece(slot, k):
        rows = pl.ds(k * piece_rows, piece_rows)
        pltpu.make_async_remote_copy(
            src_ref=ball.at[slot, rows],
            dst_ref=ball.at[slot, rows],
            send_sem=link_send.at[0, 0],
            recv_sem=piece_recv.at[slot, k],
            device_id=(oi, sibling),
            device_id_type=MESH,
        ).wait_recv()

    for k in range(3):
        for link in (PLUS, MINUS, ZED, SIBLING):
            send(oj, k, link, own=True)
    own_copy = pltpu.make_async_copy(b_hbm.at[0], ball.at[oj], local_sem.at[0])
    own_copy.start()

    lane = lax.broadcasted_iota(jnp.int32, (1, 128), 1)
    occupied = occ_ref[...].astype(jnp.float32)
    own_v = [pao_ref[pl.ds(dom_ref[0, k], 1), :] - occupied for k in range(blocks)]
    listed = jnp.zeros((1, 128), jnp.float32)
    for s in range(pair_ref.shape[1]):
        listed = listed + jnp.where(lane == pair_ref[0, s], 1.0, 0.0)
    small[oj] = jnp.concatenate(own_v + [listed] + [jnp.zeros((7 - blocks, 128), jnp.float32)], axis=0)

    def small_copy(step):
        target = lax.rem(oj + step, ROW)
        return pltpu.make_async_remote_copy(
            src_ref=small.at[oj],
            dst_ref=small.at[oj],
            send_sem=small_send.at[step],
            recv_sem=small_recv.at[step],
            device_id=(oi, target),
            device_id_type=MESH,
        )

    def small_arrival(step):
        source = lax.rem(oj + ROW - step, ROW)
        return pltpu.make_async_remote_copy(
            src_ref=small.at[source],
            dst_ref=small.at[source],
            send_sem=small_send.at[step],
            recv_sem=small_recv.at[step],
            device_id=(oi, source),
            device_id_type=MESH,
        )

    for step in range(1, ROW):
        small_copy(step).start()
    for k in range(blocks):
        vcol[k * 128:(k + 1) * 128, :] = jnp.transpose(jnp.broadcast_to(own_v[k], (128, 128)))
    own_copy.wait()
    for k in range(3):
        bt[:, k * piece_rows:(k + 1) * piece_rows] = jnp.transpose(ball[oj, k * piece_rows:(k + 1) * piece_rows, :])
    for step in range(1, ROW):
        small_arrival(step).wait_recv()

    half = dom // 2

    def amplitudes(partner, side):
        tile = small[partner]
        weight = jnp.sum(
            jnp.where(lane == partner, small[oj][blocks:blocks + 1], 0.0)
            + jnp.where(lane == oj, tile[blocks:blocks + 1], 0.0),
            axis=1, keepdims=True,
        )

        def part(h, carry):
            rows = pl.ds(pl.multiple_of(h * half, half), half)
            overlap = jnp.dot(bt[rows, :], ball[partner], preferred_element_type=jnp.float32)
            column = vcol[rows, :]
            denominator = jnp.concatenate([column + tile[k:k + 1] for k in range(blocks)], axis=1)
            mcat[rows, side * dom:(side + 1) * dom] = (overlap * (-weight) / denominator).astype(jnp.bfloat16)
            return carry

        lax.fori_loop(0, 2, part, 0)

    tile_rows = naux // 4
    per_tile = ROW // 4

    def update(chip, t):
        rows = pl.ds(pl.multiple_of(t * tile_rows, tile_rows), tile_rows)
        return rows, (
            dot_nt(ball[chip * CORES, rows, :], mcat[:, :dom])
            + dot_nt(ball[chip * CORES + 1, rows, :], mcat[:, dom:])
        )

    def process(chip, first=False):
        for side in range(CORES):
            amplitudes(chip * CORES + side, side)

        def step(t, carry):
            rows, term = update(chip, t)
            if first:
                gsum[rows, :] = term
            else:
                gsum[rows, :] += term
            return carry

        lax.fori_loop(0, 4, step, 0)

    def process_group(offsets):
        if len(offsets) == 1:
            process(chip_at(*offsets[0]))
            return

        def step(i, carry):
            chip = chip_at(*offsets[0])
            for n, offset in enumerate(offsets[1:]):
                chip = jnp.where(i == n + 1, chip_at(*offset), chip)
            process(chip)
            return carry

        lax.fori_loop(0, len(offsets), step, 0)

    def arrive(dx, dz, k):
        wait_piece(place(dx, dz), k)
        send(place(dx, dz), k, SIBLING)

    def arrived_at_sibling(dx, dz):
        other = chip_at(dx, dz) * CORES + 1 - core
        for k in range(3):
            wait_piece(other, k)

    arrived_at_sibling(0, 0)
    process(chip_at(0, 0), first=True)

    for dx, dz in ((3, 0), (1, 0), (0, 1)):
        arrive(dx, dz, 0)
    send(place(3, 0), 0, PLUS)
    send(place(3, 0), 0, ZED)
    send(place(1, 0), 0, ZED)
    for dx, dz in ((3, 0), (1, 0), (0, 1)):
        arrive(dx, dz, 1)
    send(place(0, 1), 1, PLUS)
    send(place(1, 0), 1, MINUS)
    send(place(1, 0), 1, ZED)
    for dx, dz in ((3, 0), (1, 0), (0, 1)):
        arrive(dx, dz, 2)
    send(place(0, 1), 2, PLUS)
    send(place(1, 0), 2, MINUS)
    send(place(0, 1), 2, MINUS)
    near = ((3, 0), (1, 0), (0, 1))
    for offset in near:
        arrived_at_sibling(*offset)
    process_group(near)

    arrive(2, 0, 0)
    send(place(2, 0), 0, ZED)
    arrive(2, 0, 1)
    arrive(3, 1, 0)
    arrive(3, 1, 1)
    send(place(3, 1), 1, PLUS)
    arrive(2, 0, 2)
    arrive(1, 1, 0)
    arrived_at_sibling(2, 0)
    process_group(((2, 0),))
    arrive(1, 1, 2)
    send(place(1, 1), 2, MINUS)
    arrive(3, 1, 2)
    arrive(1, 1, 1)
    diagonal = ((3, 1), (1, 1))
    for offset in diagonal:
        arrived_at_sibling(*offset)
    process_group(diagonal)
    for k in range(3):
        arrive(2, 1, k)
    arrived_at_sibling(2, 1)

    last = chip_at(2, 1)
    for side in range(CORES):
        amplitudes(last * CORES + side, side)

    def gamma_copy(target, source, where):
        return pltpu.make_async_remote_copy(
            src_ref=gout.at[pl.ds(pl.multiple_of(target * slice_rows, slice_rows), slice_rows)],
            dst_ref=gall.at[source],
            send_sem=gam_send.at[target],
            recv_sem=gam_recv.at[source],
            device_id=(oi, where),
            device_id_type=MESH,
        )

    own_slice = pltpu.make_async_copy(
        gout.at[pl.ds(pl.multiple_of(oj * slice_rows, slice_rows), slice_rows)], gall.at[oj], local_sem.at[1]
    )

    def out_copy(t):
        rows = pl.ds(pl.multiple_of(t * tile_rows, tile_rows), tile_rows)
        return pltpu.make_async_copy(gout.at[rows], gamma_out.at[0, rows], local_sem.at[2 + t])

    def finish(t, carry):
        rows, term = update(last, t)
        gout[rows, :] = (gsum[rows, :] + term).astype(jnp.bfloat16)
        out_copy(t).start()
        for k in range(per_tile):
            target = t * per_tile + k

            @pl.when(target != oj)
            def _():
                gamma_copy(target, oj, target).start()

            @pl.when(target == oj)
            def _():
                own_slice.start()
        return carry

    lax.fori_loop(0, 4, finish, 0)

    dacc[...] = jnp.zeros_like(dacc)

    def density(i, carry):
        source = (
            lax.rem(z + i // (CHIPS_X * CORES), CHIPS_Z) * CHIPS_X + lax.rem(x + i // CORES, CHIPS_X)
        ) * CORES + lax.rem(core + i, CORES)

        @pl.when(i == 0)
        def _():
            own_slice.wait()

        @pl.when(i > 0)
        def _():
            gamma_copy(source, source, source).wait_recv()

        dacc[...] += dot_nt(gall[source], ball[source])
        return carry

    lax.fori_loop(0, ROW, density, 0)
    for t in range(n_oi):
        dpart[t] = dacc[t * strip:(t + 1) * strip, :]

    def den_copy(t, row, where):
        return pltpu.make_async_remote_copy(
            src_ref=dpart.at[t],
            dst_ref=dall.at[row],
            send_sem=den_send.at[t],
            recv_sem=den_recv.at[row],
            device_id=where,
            device_id_type=MESH,
        )

    own_strip = me - first_owner

    def keep_copy():
        return pltpu.make_async_copy(dpart.at[jnp.clip(own_strip, 0, n_oi - 1)], dall.at[oi], local_sem.at[6])

    for t in range(n_oi):
        @pl.when(first_owner + t != me)
        def _():
            den_copy(t, oi, owner(t)).start()

    @pl.when(self_owner)
    def _():
        keep_copy().start()
        keep_copy().wait()

    for row in range(n_oi):
        @pl.when(jnp.logical_or(oi != row, oj != my_slice))
        def _():
            den_copy(0, row, (row, my_slice)).wait_recv()
    total = dall[0]
    for row in range(1, n_oi):
        total = total + dall[row]
    dens_out[...] = (total * (1.0 / (n_oi * ROW))).astype(jnp.bfloat16)

    for copy in started:
        copy.wait_send()
    for step in range(1, ROW):
        small_copy(step).wait_send()
    for t in range(4):
        out_copy(t).wait()

    def drain(target, carry):
        @pl.when(target != oj)
        def _():
            gamma_copy(target, oj, target).wait_send()
        return carry

    lax.fori_loop(0, ROW, drain, 0)
    for t in range(n_oi):
        @pl.when(first_owner + t != me)
        def _():
            den_copy(t, oi, owner(t)).wait_send()


def body(n_oi, b_tensor, occ_energy, dom_blocks, pair_cols, pao_energy):
    naux, dom = b_tensor.shape[1], b_tensor.shape[2]
    slice_rows = naux // ROW
    strip = slice_rows // n_oi
    vmem = pl.BlockSpec(memory_space=pltpu.VMEM)
    smem = pl.BlockSpec(memory_space=pltpu.SMEM)
    hbm = pl.BlockSpec(memory_space=pl.ANY)
    dma = pltpu.SemaphoreType.DMA
    return pl.pallas_call(
        functools.partial(kernel, n_oi),
        out_shape=(
            jax.ShapeDtypeStruct((1, naux, dom), jnp.bfloat16),
            jax.ShapeDtypeStruct((strip, naux), jnp.bfloat16),
        ),
        in_specs=[hbm, vmem, smem, smem, vmem],
        out_specs=(hbm, vmem),
        scratch_shapes=[
            pltpu.VMEM((ROW, naux, dom), jnp.bfloat16),
            pltpu.VMEM((dom, naux), jnp.bfloat16),
            pltpu.VMEM((naux, dom), jnp.float32),
            pltpu.VMEM((naux, dom), jnp.bfloat16),
            pltpu.VMEM((ROW, slice_rows, dom), jnp.bfloat16),
            pltpu.VMEM((dom, CORES * dom), jnp.bfloat16),
            pltpu.VMEM((slice_rows, naux), jnp.float32),
            pltpu.VMEM((n_oi, strip, naux), jnp.float32),
            pltpu.VMEM((n_oi, strip, naux), jnp.float32),
            pltpu.VMEM((ROW, 8, 128), jnp.float32),
            pltpu.VMEM((dom, 128), jnp.float32),
            dma((4, 24)),
            dma((ROW, 3)),
            dma((ROW,)),
            dma((ROW,)),
            dma((ROW,)),
            dma((ROW,)),
            dma((n_oi,)),
            dma((n_oi,)),
            dma((7,)),
        ],
        compiler_params=pltpu.CompilerParams(
            collective_id=0, has_side_effects=True, vmem_limit_bytes=56 * 2**20
        ),
        cost_estimate=pl.CostEstimate(
            flops=2 * naux * dom * dom * 32, bytes_accessed=4 * naux * dom, transcendentals=0
        ),
    )(b_tensor, occ_energy.reshape(1, 1), dom_blocks, pair_cols, pao_energy)


def solution(mesh):
    in_specs = (
        P(("oi", "oj"), None, None),
        P(("oi", "oj")),
        P(("oi", "oj"), None),
        P(("oi", "oj"), None),
        P(),
    )
    out_specs = (P(("oi", "oj"), None, None), P(("oi", "oj"), None))
    return jax.shard_map(
        functools.partial(body, mesh.shape["oi"]),
        mesh=mesh, in_specs=in_specs, out_specs=out_specs, check_vma=False,
    )
```

time: 894 us -> 162 us (0.18)
  the two profiles are of different devices: /device:TPU:1 before, /device:TPU:29 now
where the time goes in v1:
time: 162 us
  Pallas kernels  157 us (97%)
  local copies, waits for them, and re-layouts  3.29 us (2%)
    pallas_call x1, Pallas kernels, body(): pl.pallas_call(functools.partial(kernel, n_oi), out_shape=(jax.ShapeDtype...  157 us
    unnamed x4, local copies, waits for them, and re-layouts  3.29 us

profile of v1, /device:TPU:29, one launch (start us, length us, event | category | flops | bytes accessed | tf_op | source)
XLA Modules:
  0.0 161.9 jit_solution(3728378820249179492)
XLA Ops:
  1.3 157.3 %shard_map.68 = (bf16[1,1536,512]{2,1,0:T(8,128)(2,1)}, bf16[12,1536]{1,0:T(8,128)(2,1)}) custom-call(bf16[1,1536,512]{2,1,0:T(8,128)(2,1)} %b_hbm.1, bf16[1,1]{1,0:T(2,128)(2,1)} %bitcast.1.occ_ref, s32[1,4]{1,0:T(1,128)} %dom_ref.1, s32[1,7]{1,0:T(1,128)} %pair_ref.1, f32[64,128]{1,0:T(8,128)} %pao_ref.1), custom_call_target="tpu_custom_call" | custom-call | flops 25769803776 | bytes 3145728 | tf_op jit(solution)/shard_map/pallas_call | solution.py:377
  158.6 0.0 copy-start
  158.6 2.7 %copy.10 = bf16[1,1536,512]{2,1,0:T(8,128)(2,1)} copy(bf16[1,1536,512]{2,1,0:T(8,128)(2,1)} %get-tuple-element.4) | data formatting | bytes 3145728
  161.3 0.0 copy-done
  161.3 0.6 copy.11
Async XLA Ops:
  158.6 2.7 %copy-start = (bf16[12,1536]{1,0:T(8,128)(2,1)S(1)}, bf16[12,1536]{1,0:T(8,128)(2,1)}, u32[]{:S(2)}) copy-start(bf16[12,1536]{1,0:T(8,128)(2,1)} %get-tuple-element.5) | copy-start | bytes 110596

commit v2 on v1

--- a/solution.py
+++ b/solution.py
@@ -159,10 +159,18 @@
         lax.fori_loop(0, 2, part, 0)
 
     tile_rows = naux // 4
-    per_tile = ROW // 4
-
-    def update(chip, t):
-        rows = pl.ds(pl.multiple_of(t * tile_rows, tile_rows), tile_rows)
+    chips = ROW // CORES
+    chip_rows = naux // chips
+    ring = ((2, 1), (1, 1), (3, 1), (2, 0), (0, 1), (1, 0), (3, 0), (0, 0))
+
+    def pick(i, offsets):
+        chip = chip_at(*offsets[0])
+        for n, offset in enumerate(offsets[1:]):
+            chip = jnp.where(i == n + 1, chip_at(*offset), chip)
+        return chip
+
+    def update(chip, t, size=tile_rows):
+        rows = pl.ds(pl.multiple_of(t * size, size), size)
         return rows, (
             dot_nt(ball[chip * CORES, rows, :], mcat[:, :dom])
             + dot_nt(ball[chip * CORES + 1, rows, :], mcat[:, dom:])
@@ -188,10 +196,7 @@
             return
 
         def step(i, carry):
-            chip = chip_at(*offsets[0])
-            for n, offset in enumerate(offsets[1:]):
-                chip = jnp.where(i == n + 1, chip_at(*offset), chip)
-            process(chip)
+            process(pick(i, offsets))
             return carry
 
         lax.fori_loop(0, len(offsets), step, 0)
@@ -269,15 +274,16 @@
     )
 
     def out_copy(t):
-        rows = pl.ds(pl.multiple_of(t * tile_rows, tile_rows), tile_rows)
-        return pltpu.make_async_copy(gout.at[rows], gamma_out.at[0, rows], local_sem.at[2 + t])
-
-    def finish(t, carry):
-        rows, term = update(last, t)
+        rows = pl.ds(pl.multiple_of(t * chip_rows, chip_rows), chip_rows)
+        return pltpu.make_async_copy(gout.at[rows], gamma_out.at[0, rows], local_sem.at[3 + t])
+
+    def finish(i, carry):
+        chip = pick(i, ring)
+        rows, term = update(last, chip, chip_rows)
         gout[rows, :] = (gsum[rows, :] + term).astype(jnp.bfloat16)
-        out_copy(t).start()
-        for k in range(per_tile):
-            target = t * per_tile + k
+        out_copy(chip).start()
+        for k in range(CORES):
+            target = chip * CORES + lax.rem(core + k, CORES)
 
             @pl.when(target != oj)
             def _():
@@ -288,20 +294,18 @@
                 own_slice.start()
         return carry
 
-    lax.fori_loop(0, 4, finish, 0)
+    lax.fori_loop(0, chips, finish, 0)
 
     dacc[...] = jnp.zeros_like(dacc)
 
     def density(i, carry):
-        source = (
-            lax.rem(z + i // (CHIPS_X * CORES), CHIPS_Z) * CHIPS_X + lax.rem(x + i // CORES, CHIPS_X)
-        ) * CORES + lax.rem(core + i, CORES)
-
-        @pl.when(i == 0)
+        source = pick(i // CORES, ring) * CORES + lax.rem(core + i, CORES)
+
+        @pl.when(source == oj)
         def _():
             own_slice.wait()
 
-        @pl.when(i > 0)
+        @pl.when(source != oj)
         def _():
             gamma_copy(source, source, source).wait_recv()
 
@@ -309,8 +313,13 @@
         return carry
 
     lax.fori_loop(0, ROW, density, 0)
+    groups = 4
+    lanes = naux // groups
     for t in range(n_oi):
-        dpart[t] = dacc[t * strip:(t + 1) * strip, :]
+        rows = dacc[t * strip:(t + 1) * strip, :]
+        dpart[t] = jnp.concatenate(
+            [rows[:, g * lanes:(g + 1) * lanes] for g in range(groups)], axis=0
+        ).astype(jnp.bfloat16)
 
     def den_copy(t, row, where):
         return pltpu.make_async_remote_copy(
@@ -325,7 +334,7 @@
     own_strip = me - first_owner
 
     def keep_copy():
-        return pltpu.make_async_copy(dpart.at[jnp.clip(own_strip, 0, n_oi - 1)], dall.at[oi], local_sem.at[6])
+        return pltpu.make_async_copy(dpart.at[jnp.clip(own_strip, 0, n_oi - 1)], dall.at[oi], local_sem.at[2])
 
     for t in range(n_oi):
         @pl.when(first_owner + t != me)
@@ -341,16 +350,19 @@
         @pl.when(jnp.logical_or(oi != row, oj != my_slice))
         def _():
             den_copy(0, row, (row, my_slice)).wait_recv()
-    total = dall[0]
+    total = dall[0].astype(jnp.float32)
     for row in range(1, n_oi):
-        total = total + dall[row]
-    dens_out[...] = (total * (1.0 / (n_oi * ROW))).astype(jnp.bfloat16)
+        total = total + dall[row].astype(jnp.float32)
+    total = total * (1.0 / (n_oi * ROW))
+    dens_out[...] = jnp.concatenate(
+        [total[g * strip:(g + 1) * strip] for g in range(groups)], axis=1
+    ).astype(jnp.bfloat16)
 
     for copy in started:
         copy.wait_send()
     for step in range(1, ROW):
         small_copy(step).wait_send()
-    for t in range(4):
+    for t in range(chips):
         out_copy(t).wait()
 
     def drain(target, carry):
@@ -390,8 +402,8 @@
             pltpu.VMEM((ROW, slice_rows, dom), jnp.bfloat16),
             pltpu.VMEM((dom, CORES * dom), jnp.bfloat16),
             pltpu.VMEM((slice_rows, naux), jnp.float32),
-            pltpu.VMEM((n_oi, strip, naux), jnp.float32),
-            pltpu.VMEM((n_oi, strip, naux), jnp.float32),
+            pltpu.VMEM((n_oi, 4 * strip, naux // 4), jnp.bfloat16),
+            pltpu.VMEM((n_oi, 4 * strip, naux // 4), jnp.bfloat16),
             pltpu.VMEM((ROW, 8, 128), jnp.float32),
             pltpu.VMEM((dom, 128), jnp.float32),
             dma((4, 24)),
@@ -402,7 +414,7 @@
             dma((ROW,)),
             dma((n_oi,)),
             dma((n_oi,)),
-            dma((7,)),
+            dma((11,)),
         ],
         compiler_params=pltpu.CompilerParams(
             collective_id=0, has_side_effects=True, vmem_limit_bytes=56 * 2**20

time: 162 us -> 149 us (0.920)
  the two profiles are of different devices: /device:TPU:29 before, /device:TPU:1 now
where the time goes in v2:
time: 149 us
  Pallas kernels  144 us (97%)
  local copies, waits for them, and re-layouts  3.29 us (2%)
    pallas_call x1, Pallas kernels, body(): pl.pallas_call(functools.partial(kernel, n_oi), out_shape=(jax.ShapeDtype...  144 us
    unnamed x4, local copies, waits for them, and re-layouts  3.29 us

profile of v2, /device:TPU:1, one launch (start us, length us, event | category | flops | bytes accessed | tf_op | source)
XLA Modules:
  0.0 149.0 jit_solution(16058640272817778187)
XLA Ops:
  1.3 144.4 %shard_map.68 = (bf16[1,1536,512]{2,1,0:T(8,128)(2,1)}, bf16[12,1536]{1,0:T(8,128)(2,1)}) custom-call(bf16[1,1536,512]{2,1,0:T(8,128)(2,1)} %b_hbm.1, bf16[1,1]{1,0:T(2,128)(2,1)} %bitcast.1.occ_ref, s32[1,4]{1,0:T(1,128)} %dom_ref.1, s32[1,7]{1,0:T(1,128)} %pair_ref.1, f32[64,128]{1,0:T(8,128)} %pao_ref.1), custom_call_target="tpu_custom_call" | custom-call | flops 25769803776 | bytes 3145728 | tf_op jit(solution)/shard_map/pallas_call | solution.py:389
  145.7 0.0 copy-start
  145.7 2.7 %copy.10 = bf16[1,1536,512]{2,1,0:T(8,128)(2,1)} copy(bf16[1,1536,512]{2,1,0:T(8,128)(2,1)} %get-tuple-element.4) | data formatting | bytes 3145728
  148.3 0.0 copy-done
  148.3 0.6 copy.11
Async XLA Ops:
  145.7 2.7 %copy-start = (bf16[12,1536]{1,0:T(8,128)(2,1)S(1)}, bf16[12,1536]{1,0:T(8,128)(2,1)}, u32[]{:S(2)}) copy-start(bf16[12,1536]{1,0:T(8,128)(2,1)} %get-tuple-element.5) | copy-start | bytes 110596

commit v3 on v2

v3 whole, which is shorter than its diff:
```python
import functools

import jax
import jax.numpy as jnp
from jax import lax
from jax.experimental import pallas as pl
from jax.experimental.pallas import tpu as pltpu
from jax.sharding import PartitionSpec as P

MESH = pl.DeviceIdType.MESH
PLUS, MINUS, ZED, SIBLING = range(4)
CHIPS_X, CHIPS_Z, CORES = 4, 2, 2
ROW = CHIPS_X * CHIPS_Z * CORES
HEAD = 16


def dot_nt(lhs, rhs):
    return lax.dot_general(lhs, rhs, (((1,), (1,)), ((), ())), preferred_element_type=jnp.float32)


def kernel(
    n_oi, b_hbm, occ_ref, dom_ref, pair_ref, pao_ref, gamma_out, dens_out,
    ball, bt, gsum, gout, gall, mcat, dacc, dpart, dall, vcol,
    link_send, piece_recv, gam_send, gam_recv, den_send, den_recv, local_sem, known,
):
    naux, dom = b_hbm.shape[1], b_hbm.shape[2]
    blocks = dom // 128
    piece_rows = naux // 3
    slice_rows = naux // ROW
    strip = slice_rows // n_oi
    oi, oj = lax.axis_index("oi"), lax.axis_index("oj")
    core, x, z = lax.rem(oj, 2), lax.rem(oj // 2, CHIPS_X), oj // (CHIPS_X * CORES)

    def chip_at(dx, dz):
        return lax.rem(z + dz, CHIPS_Z) * CHIPS_X + lax.rem(x + dx, CHIPS_X)

    def place(dx, dz):
        return chip_at(dx, dz) * CORES + core

    sibling = oj + 1 - 2 * core
    link_to = {PLUS: place(1, 0), MINUS: place(3, 0), ZED: place(0, 1), SIBLING: sibling}

    def slice_of(position):
        return (
            lax.rem(position // CORES, CHIPS_X) * (CORES * CHIPS_Z)
            + lax.rem(position, CORES) * CHIPS_Z
            + position // (CHIPS_X * CORES)
        )

    def position_of(part):
        return (
            lax.rem(part, CHIPS_Z) * CHIPS_X + part // (CORES * CHIPS_Z)
        ) * CORES + lax.rem(part // CHIPS_Z, CORES)

    me = oi * ROW + oj
    first_owner = slice_of(oj) * n_oi
    my_slice = position_of(me // n_oi)
    self_owner = jnp.logical_and(first_owner <= me, me < first_owner + n_oi)

    def owner(t):
        flat = first_owner + t
        return flat // ROW, lax.rem(flat, ROW)

    own_copy = pltpu.make_async_copy(b_hbm.at[0], ball.at[oj, pl.ds(HEAD, naux)], local_sem.at[0])
    own_copy.start()

    lane = lax.broadcasted_iota(jnp.int32, (1, dom), 1)
    occupied = occ_ref[...].astype(jnp.float32)
    own_v = [pao_ref[pl.ds(dom_ref[0, k], 1), :] - occupied for k in range(blocks)]
    rest = jnp.concatenate(own_v, axis=1)
    head = []
    for _ in range(3):
        head.append(rest.astype(jnp.bfloat16).astype(jnp.float32))
        rest = rest - head[-1]
    listed = jnp.zeros((1, dom), jnp.float32)
    for s in range(pair_ref.shape[1]):
        listed = listed + jnp.where(lane == pair_ref[0, s], 1.0, 0.0)
    head += [listed, jnp.zeros((HEAD - 4, dom), jnp.float32)]
    ball[oj, 0:HEAD, :] = jnp.concatenate(head, axis=0).astype(jnp.bfloat16)
    own_copy.wait()

    y_index, z_high = oi // 2, lax.rem(oi, 2)
    beside = [(oi, link_to[link]) for link in range(4)]
    rows_beside = [
        (lax.rem(y_index + 1, 4) * 2 + z_high, oj),
        (lax.rem(y_index + 3, 4) * 2 + z_high, oj),
        (oi + 1 - 2 * z_high, oj),
    ]
    barrier = pltpu.get_barrier_semaphore()
    for device in beside + rows_beside:
        pl.semaphore_signal(barrier, inc=1, device_id=device, device_id_type=MESH)
    pl.semaphore_wait(barrier, len(beside + rows_beside))

    def tell(stage):
        for device in rows_beside:
            pl.semaphore_signal(known.at[stage], inc=1, device_id=device, device_id_type=MESH)

    def hear(stage):
        pl.semaphore_wait(known.at[stage], len(rows_beside))

    counts = [0, 0, 0, 0]
    started = []

    def piece(slot, k):
        if k == 0:
            return ball.at[slot, pl.ds(0, HEAD + piece_rows)]
        return ball.at[slot, pl.ds(HEAD + k * piece_rows, piece_rows)]

    def send(slot, k, link):
        copy = pltpu.make_async_remote_copy(
            src_ref=piece(slot, k),
            dst_ref=piece(slot, k),
            send_sem=link_send.at[link, counts[link]],
            recv_sem=piece_recv.at[slot, k],
            device_id=(oi, link_to[link]),
            device_id_type=MESH,
        )
        counts[link] += 1
        copy.start()
        started.append(copy)

    def wait_piece(slot, k):
        pltpu.make_async_remote_copy(
            src_ref=piece(slot, k),
            dst_ref=piece(slot, k),
            send_sem=link_send.at[0, 0],
            recv_sem=piece_recv.at[slot, k],
            device_id=(oi, sibling),
            device_id_type=MESH,
        ).wait_recv()

    for k in range(3):
        for link in (PLUS, MINUS, ZED, SIBLING):
            send(oj, k, link)

    for k in range(blocks):
        vcol[k * 128:(k + 1) * 128, :] = jnp.transpose(jnp.broadcast_to(own_v[k], (128, 128)))
    for k in range(3):
        bt[:, k * piece_rows:(k + 1) * piece_rows] = jnp.transpose(
            ball[oj, HEAD + k * piece_rows:HEAD + (k + 1) * piece_rows, :]
        )

    def block(slot, start=0, size=naux):
        return ball[slot, pl.ds(pl.multiple_of(HEAD + start, HEAD), size), :]

    def amplitudes(partner, side):
        own_head = ball[oj, 0:HEAD, :].astype(jnp.float32)
        its_head = ball[partner, 0:HEAD, :].astype(jnp.float32)
        energies = its_head[0:1] + its_head[1:2] + its_head[2:3]
        weight = jnp.sum(
            jnp.where(lane == partner, own_head[3:4], 0.0) + jnp.where(lane == oj, its_head[3:4], 0.0),
            axis=1, keepdims=True,
        )
        overlap = jnp.dot(bt[...], block(partner), preferred_element_type=jnp.float32)
        column = vcol[...]
        denominator = jnp.concatenate(
            [column + energies[:, k * 128:(k + 1) * 128] for k in range(blocks)], axis=1
        )
        mcat[:, pl.ds(pl.multiple_of(side * dom, dom), dom)] = (
            overlap * (-weight) / denominator
        ).astype(jnp.bfloat16)

    half_rows = naux // 2

    def pick(i, offsets):
        chip = chip_at(*offsets[0])
        for n, offset in enumerate(offsets[1:]):
            chip = jnp.where(i == n + 1, chip_at(*offset), chip)
        return chip

    def update(chip, start=0, size=naux):
        return (
            dot_nt(block(chip * CORES, start, size), mcat[:, :dom])
            + dot_nt(block(chip * CORES + 1, start, size), mcat[:, dom:])
        )

    def process(chip, first=False):
        for side in range(CORES):
            amplitudes(chip * CORES + side, side)

        if first:
            gsum[...] = update(chip)
        else:
            gsum[...] += update(chip)

    def process_group(offsets):
        if len(offsets) == 1:
            process(chip_at(*offsets[0]))
            return

        def step(i, carry):
            process(pick(i, offsets))
            return carry

        lax.fori_loop(0, len(offsets), step, 0)

    def arrive(dx, dz, k):
        wait_piece(place(dx, dz), k)
        send(place(dx, dz), k, SIBLING)

    def arrived_at_sibling(dx, dz):
        other = chip_at(dx, dz) * CORES + 1 - core
        for k in range(3):
            wait_piece(other, k)

    arrived_at_sibling(0, 0)
    process(chip_at(0, 0), first=True)

    for dx, dz in ((3, 0), (1, 0), (0, 1)):
        arrive(dx, dz, 0)
    send(place(3, 0), 0, PLUS)
    send(place(3, 0), 0, ZED)
    send(place(1, 0), 0, ZED)
    for dx, dz in ((3, 0), (1, 0), (0, 1)):
        arrive(dx, dz, 1)
    send(place(0, 1), 1, PLUS)
    send(place(1, 0), 1, MINUS)
    send(place(1, 0), 1, ZED)
    for dx, dz in ((3, 0), (1, 0), (0, 1)):
        arrive(dx, dz, 2)
    send(place(0, 1), 2, PLUS)
    send(place(1, 0), 2, MINUS)
    send(place(0, 1), 2, MINUS)
    near = ((3, 0), (1, 0), (0, 1))
    for offset in near:
        arrived_at_sibling(*offset)
    process_group(near)

    arrive(2, 0, 0)
    send(place(2, 0), 0, ZED)
    arrive(2, 0, 1)
    arrive(3, 1, 0)
    arrive(3, 1, 1)
    send(place(3, 1), 1, PLUS)
    arrive(2, 0, 2)
    arrive(1, 1, 0)
    arrived_at_sibling(2, 0)
    process_group(((2, 0),))
    arrive(1, 1, 2)
    send(place(1, 1), 2, MINUS)
    arrive(3, 1, 2)
    arrive(1, 1, 1)
    diagonal = ((3, 1), (1, 1))
    for offset in diagonal:
        arrived_at_sibling(*offset)
    process_group(diagonal)
    last = chip_at(2, 1)
    for k in range(3):
        arrive(2, 1, k)

    amplitudes(last * CORES + core, core)
    arrived_at_sibling(2, 1)
    tell(0)
    amplitudes(last * CORES + 1 - core, 1 - core)

    def slice_rows_of(position):
        return pl.ds(pl.multiple_of(slice_of(position) * slice_rows, slice_rows), slice_rows)

    def gamma_copy(target, source, where):
        return pltpu.make_async_remote_copy(
            src_ref=gout.at[slice_rows_of(target)],
            dst_ref=gall.at[source],
            send_sem=gam_send.at[target],
            recv_sem=gam_recv.at[source],
            device_id=(oi, where),
            device_id_type=MESH,
        )

    own_slice = pltpu.make_async_copy(gout.at[slice_rows_of(oj)], gall.at[oj], local_sem.at[1])

    def out_copy(i):
        rows = pl.ds(pl.multiple_of(i * half_rows, half_rows), half_rows)
        return pltpu.make_async_copy(gout.at[rows], gamma_out.at[0, rows], local_sem.at[3 + i])

    ring = ((2, 1), (2, 0), (1, 1), (3, 1), (1, 0), (3, 0), (0, 1), (0, 0))

    def finish(i, carry):
        part = lax.rem(x // 2 + 1 + i, 2)
        rows = pl.ds(pl.multiple_of(part * half_rows, half_rows), half_rows)
        term = update(last, part * half_rows, half_rows)
        gout[rows, :] = (gsum[rows, :] + term).astype(jnp.bfloat16)

        def leave(n, inner):
            chip = pick(n, ring)
            for k in range(CORES):
                target = chip * CORES + lax.rem(core + k, CORES)
                here = lax.rem(chip, CHIPS_X) // 2 == part

                @pl.when(jnp.logical_and(here, target != oj))
                def _():
                    gamma_copy(target, oj, target).start()

                @pl.when(jnp.logical_and(here, target == oj))
                def _():
                    own_slice.start()
            return inner

        lax.fori_loop(0, ROW // CORES, leave, 0)
        out_copy(part).start()
        return carry

    lax.fori_loop(0, 2, finish, 0)
    hear(0)
    tell(1)

    dacc[...] = jnp.zeros_like(dacc)

    def density(i, carry):
        chip = pick(i, ring)
        for k in range(CORES):
            source = chip * CORES + k

            @pl.when(source == oj)
            def _():
                own_slice.wait()

            @pl.when(source != oj)
            def _():
                gamma_copy(source, source, source).wait_recv()

        source = chip * CORES
        dacc[...] += (
            dot_nt(gall[source], block(source)) + dot_nt(gall[source + 1], block(source + 1))
        )
        return carry

    lax.fori_loop(0, 3, density, 0)
    hear(1)
    tell(2)
    lax.fori_loop(3, ROW // CORES, density, 0)
    hear(2)
    groups = 4
    lanes = naux // groups
    for t in range(n_oi):
        rows = dacc[t * strip:(t + 1) * strip, :]
        dpart[t] = jnp.concatenate(
            [rows[:, g * lanes:(g + 1) * lanes] for g in range(groups)], axis=0
        ).astype(jnp.bfloat16)

    def den_copy(t, row, where):
        return pltpu.make_async_remote_copy(
            src_ref=dpart.at[t],
            dst_ref=dall.at[row],
            send_sem=den_send.at[t],
            recv_sem=den_recv.at[row],
            device_id=where,
            device_id_type=MESH,
        )

    own_strip = me - first_owner

    def keep_copy():
        return pltpu.make_async_copy(dpart.at[jnp.clip(own_strip, 0, n_oi - 1)], dall.at[oi], local_sem.at[2])

    for t in range(n_oi):
        @pl.when(first_owner + t != me)
        def _():
            den_copy(t, oi, owner(t)).start()

    @pl.when(self_owner)
    def _():
        keep_copy().start()
        keep_copy().wait()

    for row in range(n_oi):
        @pl.when(jnp.logical_or(oi != row, oj != my_slice))
        def _():
            den_copy(0, row, (row, my_slice)).wait_recv()
    total = dall[0].astype(jnp.float32)
    for row in range(1, n_oi):
        total = total + dall[row].astype(jnp.float32)
    total = total * (1.0 / (n_oi * ROW))
    dens_out[...] = jnp.concatenate(
        [total[g * strip:(g + 1) * strip] for g in range(groups)], axis=1
    ).astype(jnp.bfloat16)

    for copy in started:
        copy.wait_send()
    for t in range(2):
        out_copy(t).wait()

    def drain(target, carry):
        @pl.when(target != oj)
        def _():
            gamma_copy(target, oj, target).wait_send()
        return carry

    lax.fori_loop(0, ROW, drain, 0)
    for t in range(n_oi):
        @pl.when(first_owner + t != me)
        def _():
            den_copy(t, oi, owner(t)).wait_send()


def body(n_oi, b_tensor, occ_energy, dom_blocks, pair_cols, pao_energy):
    naux, dom = b_tensor.shape[1], b_tensor.shape[2]
    slice_rows = naux // ROW
    strip = slice_rows // n_oi
    vmem = pl.BlockSpec(memory_space=pltpu.VMEM)
    smem = pl.BlockSpec(memory_space=pltpu.SMEM)
    hbm = pl.BlockSpec(memory_space=pl.ANY)
    dma = pltpu.SemaphoreType.DMA
    return pl.pallas_call(
        functools.partial(kernel, n_oi),
        out_shape=(
            jax.ShapeDtypeStruct((1, naux, dom), jnp.bfloat16),
            jax.ShapeDtypeStruct((strip, naux), jnp.bfloat16),
        ),
        in_specs=[hbm, vmem, smem, smem, vmem],
        out_specs=(hbm, vmem),
        scratch_shapes=[
            pltpu.VMEM((ROW, HEAD + naux, dom), jnp.bfloat16),
            pltpu.VMEM((dom, naux), jnp.bfloat16),
            pltpu.VMEM((naux, dom), jnp.float32),
            pltpu.VMEM((naux, dom), jnp.bfloat16),
            pltpu.VMEM((ROW, slice_rows, dom), jnp.bfloat16),
            pltpu.VMEM((dom, CORES * dom), jnp.bfloat16),
            pltpu.VMEM((slice_rows, naux), jnp.float32),
            pltpu.VMEM((n_oi, 4 * strip, naux // 4), jnp.bfloat16),
            pltpu.VMEM((n_oi, 4 * strip, naux // 4), jnp.bfloat16),
            pltpu.VMEM((dom, 128), jnp.float32),
            dma((4, 24)),
            dma((ROW, 3)),
            dma((ROW,)),
            dma((ROW,)),
            dma((n_oi,)),
            dma((n_oi,)),
            dma((5,)),
            pltpu.SemaphoreType.REGULAR((3,)),
        ],
        compiler_params=pltpu.CompilerParams(
            collective_id=0, has_side_effects=True, vmem_limit_bytes=56 * 2**20
        ),
        cost_estimate=pl.CostEstimate(
            flops=2 * naux * dom * dom * 32, bytes_accessed=4 * naux * dom, transcendentals=0
        ),
    )(b_tensor, occ_energy.reshape(1, 1), dom_blocks, pair_cols, pao_energy)


def solution(mesh):
    in_specs = (
        P(("oi", "oj"), None, None),
        P(("oi", "oj")),
        P(("oi", "oj"), None),
        P(("oi", "oj"), None),
        P(),
    )
    out_specs = (P(("oi", "oj"), None, None), P(("oi", "oj"), None))
    return jax.shard_map(
        functools.partial(body, mesh.shape["oi"]),
        mesh=mesh, in_specs=in_specs, out_specs=out_specs, check_vma=False,
    )
```

time: 149 us -> 136 us (0.913)
  Pallas kernels: 144 us -> 131 us
    pallas_call x1, Pallas kernels: 144 us -> 131 us  [body(): pl.pallas_call(functools.partial(kernel, n_oi), out_shape=(jax.ShapeDtype...]
where the time goes in v3:
time: 136 us; the launch traced here: 135 us
  Pallas kernels  131 us (96%)
  local copies, waits for them, and re-layouts  3.29 us (2%)
    pallas_call x1, Pallas kernels, body(): pl.pallas_call(functools.partial(kernel, n_oi), out_shape=(jax.ShapeDtype...  131 us
    unnamed x4, local copies, waits for them, and re-layouts  3.29 us

profile of v3, /device:TPU:1, one launch (start us, length us, event | category | flops | bytes accessed | tf_op | source)
XLA Modules:
  0.0 135.4 jit_solution(6074394760304660826)
XLA Ops:
  1.3 130.8 %shard_map.68 = (bf16[1,1536,512]{2,1,0:T(8,128)(2,1)}, bf16[12,1536]{1,0:T(8,128)(2,1)}) custom-call(bf16[1,1536,512]{2,1,0:T(8,128)(2,1)} %b_hbm.1, bf16[1,1]{1,0:T(2,128)(2,1)} %bitcast.1.occ_ref, s32[1,4]{1,0:T(1,128)} %dom_ref.1, s32[1,7]{1,0:T(1,128)} %pair_ref.1, f32[64,128]{1,0:T(8,128)} %pao_ref.1), custom_call_target="tpu_custom_call" | custom-call | flops 25769803776 | bytes 3145728 | tf_op jit(solution)/shard_map/pallas_call | solution.py:403
  132.1 0.0 copy-start
  132.1 2.7 %copy.10 = bf16[1,1536,512]{2,1,0:T(8,128)(2,1)} copy(bf16[1,1536,512]{2,1,0:T(8,128)(2,1)} %get-tuple-element.4) | data formatting | bytes 3145728
  134.8 0.0 copy-done
  134.8 0.6 copy.11
Async XLA Ops:
  132.1 2.7 %copy-start = (bf16[12,1536]{1,0:T(8,128)(2,1)S(1)}, bf16[12,1536]{1,0:T(8,128)(2,1)}, u32[]{:S(2)}) copy-start(bf16[12,1536]{1,0:T(8,128)(2,1)} %get-tuple-element.5) | copy-start | bytes 110596

commit v4 on v3

--- a/solution.py
+++ b/solution.py
@@ -61,6 +61,16 @@
         flat = first_owner + t
         return flat // ROW, lax.rem(flat, ROW)
 
+    y_index, z_high = oi // 2, lax.rem(oi, 2)
+    beside = [(oi, link_to[link]) for link in range(4)]
+    rows_beside = [
+        (lax.rem(y_index + 1, 4) * 2 + z_high, oj),
+        (lax.rem(y_index + 3, 4) * 2 + z_high, oj),
+        (oi + 1 - 2 * z_high, oj),
+    ]
+    barrier = pltpu.get_barrier_semaphore()
+    for device in beside + rows_beside:
+        pl.semaphore_signal(barrier, inc=1, device_id=device, device_id_type=MESH)
     own_copy = pltpu.make_async_copy(b_hbm.at[0], ball.at[oj, pl.ds(HEAD, naux)], local_sem.at[0])
     own_copy.start()
 
@@ -79,16 +89,6 @@
     ball[oj, 0:HEAD, :] = jnp.concatenate(head, axis=0).astype(jnp.bfloat16)
     own_copy.wait()
 
-    y_index, z_high = oi // 2, lax.rem(oi, 2)
-    beside = [(oi, link_to[link]) for link in range(4)]
-    rows_beside = [
-        (lax.rem(y_index + 1, 4) * 2 + z_high, oj),
-        (lax.rem(y_index + 3, 4) * 2 + z_high, oj),
-        (oi + 1 - 2 * z_high, oj),
-    ]
-    barrier = pltpu.get_barrier_semaphore()
-    for device in beside + rows_beside:
-        pl.semaphore_signal(barrier, inc=1, device_id=device, device_id_type=MESH)
     pl.semaphore_wait(barrier, len(beside + rows_beside))
 
     def tell(stage):
@@ -302,32 +302,36 @@
     lax.fori_loop(0, 2, finish, 0)
     hear(0)
     tell(1)
+    for copy in started:
+        copy.wait_send()
 
     dacc[...] = jnp.zeros_like(dacc)
 
     def density(i, carry):
-        chip = pick(i, ring)
-        for k in range(CORES):
-            source = chip * CORES + k
-
-            @pl.when(source == oj)
-            def _():
-                own_slice.wait()
-
-            @pl.when(source != oj)
-            def _():
-                gamma_copy(source, source, source).wait_recv()
-
-        source = chip * CORES
-        dacc[...] += (
-            dot_nt(gall[source], block(source)) + dot_nt(gall[source + 1], block(source + 1))
-        )
+        for n in range(2):
+            chip = pick(2 * i + n, ring)
+            for k in range(CORES):
+                source = chip * CORES + k
+
+                @pl.when(source == oj)
+                def _():
+                    own_slice.wait()
+
+                @pl.when(source != oj)
+                def _():
+                    gamma_copy(source, source, source).wait_recv()
+
+        terms = [
+            dot_nt(gall[pick(2 * i + n, ring) * CORES + k], block(pick(2 * i + n, ring) * CORES + k))
+            for n in range(2) for k in range(CORES)
+        ]
+        dacc[...] += (terms[0] + terms[1]) + (terms[2] + terms[3])
         return carry
 
-    lax.fori_loop(0, 3, density, 0)
+    lax.fori_loop(0, 1, density, 0)
     hear(1)
     tell(2)
-    lax.fori_loop(3, ROW // CORES, density, 0)
+    lax.fori_loop(1, ROW // CORES // 2, density, 0)
     hear(2)
     groups = 4
     lanes = naux // groups
@@ -360,6 +364,19 @@
     @pl.when(self_owner)
     def _():
         keep_copy().start()
+
+    for t in range(2):
+        out_copy(t).wait()
+
+    def drain(target, carry):
+        @pl.when(target != oj)
+        def _():
+            gamma_copy(target, oj, target).wait_send()
+        return carry
+
+    lax.fori_loop(0, ROW, drain, 0)
+    @pl.when(self_owner)
+    def _():
         keep_copy().wait()
 
     for row in range(n_oi):
@@ -374,18 +391,6 @@
         [total[g * strip:(g + 1) * strip] for g in range(groups)], axis=1
     ).astype(jnp.bfloat16)
 
-    for copy in started:
-        copy.wait_send()
-    for t in range(2):
-        out_copy(t).wait()
-
-    def drain(target, carry):
-        @pl.when(target != oj)
-        def _():
-            gamma_copy(target, oj, target).wait_send()
-        return carry
-
-    lax.fori_loop(0, ROW, drain, 0)
     for t in range(n_oi):
         @pl.when(first_owner + t != me)
         def _():

time: 136 us -> 134 us (0.985)
  Pallas kernels: 131 us -> 129 us
    pallas_call x1, Pallas kernels: 131 us -> 129 us  [body(): pl.pallas_call(functools.partial(kernel, n_oi), out_shape=(jax.ShapeDtype...]
where the time goes in v4:
time: 134 us
  Pallas kernels  129 us (96%)
  local copies, waits for them, and re-layouts  3.29 us (2%)
    pallas_call x1, Pallas kernels, body(): pl.pallas_call(functools.partial(kernel, n_oi), out_shape=(jax.ShapeDtype...  129 us
    unnamed x4, local copies, waits for them, and re-layouts  3.29 us

profile of v4, /device:TPU:1, one launch (start us, length us, event | category | flops | bytes accessed | tf_op | source)
XLA Modules:
  0.0 133.7 jit_solution(17129081238570025017)
XLA Ops:
  1.3 129.1 %shard_map.68 = (bf16[1,1536,512]{2,1,0:T(8,128)(2,1)}, bf16[12,1536]{1,0:T(8,128)(2,1)}) custom-call(bf16[1,1536,512]{2,1,0:T(8,128)(2,1)} %b_hbm.1, bf16[1,1]{1,0:T(2,128)(2,1)} %bitcast.1.occ_ref, s32[1,4]{1,0:T(1,128)} %dom_ref.1, s32[1,7]{1,0:T(1,128)} %pair_ref.1, f32[64,128]{1,0:T(8,128)} %pao_ref.1), custom_call_target="tpu_custom_call" | custom-call | flops 25769803776 | bytes 3145728 | tf_op jit(solution)/shard_map/pallas_call | solution.py:408
  130.4 0.0 copy-start
  130.4 2.7 %copy.10 = bf16[1,1536,512]{2,1,0:T(8,128)(2,1)} copy(bf16[1,1536,512]{2,1,0:T(8,128)(2,1)} %get-tuple-element.4) | data formatting | bytes 3145728
  133.1 0.0 copy-done
  133.1 0.6 copy.11
Async XLA Ops:
  130.4 2.7 %copy-start = (bf16[12,1536]{1,0:T(8,128)(2,1)S(1)}, bf16[12,1536]{1,0:T(8,128)(2,1)}, u32[]{:S(2)}) copy-start(bf16[12,1536]{1,0:T(8,128)(2,1)} %get-tuple-element.5) | copy-start | bytes 110596

commit v5 on v4

--- a/solution.py
+++ b/solution.py
@@ -19,8 +19,8 @@
 
 
 def kernel(
-    n_oi, b_hbm, occ_ref, dom_ref, pair_ref, pao_ref, gamma_out, dens_out,
-    ball, bt, gsum, gout, gall, mcat, dacc, dpart, dall, vcol,
+    n_oi, b_hbm, occ_ref, dom_hbm, pair_hbm, pao_hbm, gamma_out, dens_out,
+    dom_ref, pair_ref, pao_ref, ball, bt, gsum, gout, gall, mcat, dacc, dpart, dall, vcol,
     link_send, piece_recv, gam_send, gam_recv, den_send, den_recv, local_sem, known,
 ):
     naux, dom = b_hbm.shape[1], b_hbm.shape[2]
@@ -72,7 +72,15 @@
     for device in beside + rows_beside:
         pl.semaphore_signal(barrier, inc=1, device_id=device, device_id_type=MESH)
     own_copy = pltpu.make_async_copy(b_hbm.at[0], ball.at[oj, pl.ds(HEAD, naux)], local_sem.at[0])
+    fetches = [
+        pltpu.make_async_copy(source, target, local_sem.at[5 + n])
+        for n, (source, target) in enumerate(((dom_hbm, dom_ref), (pair_hbm, pair_ref), (pao_hbm, pao_ref)))
+    ]
+    for fetch in fetches:
+        fetch.start()
     own_copy.start()
+    for fetch in fetches:
+        fetch.wait()
 
     lane = lax.broadcasted_iota(jnp.int32, (1, dom), 1)
     occupied = occ_ref[...].astype(jnp.float32)
@@ -402,7 +410,6 @@
     slice_rows = naux // ROW
     strip = slice_rows // n_oi
     vmem = pl.BlockSpec(memory_space=pltpu.VMEM)
-    smem = pl.BlockSpec(memory_space=pltpu.SMEM)
     hbm = pl.BlockSpec(memory_space=pl.ANY)
     dma = pltpu.SemaphoreType.DMA
     return pl.pallas_call(
@@ -411,9 +418,12 @@
             jax.ShapeDtypeStruct((1, naux, dom), jnp.bfloat16),
             jax.ShapeDtypeStruct((strip, naux), jnp.bfloat16),
         ),
-        in_specs=[hbm, vmem, smem, smem, vmem],
+        in_specs=[hbm, vmem, hbm, hbm, hbm],
         out_specs=(hbm, vmem),
         scratch_shapes=[
+            pltpu.SMEM(dom_blocks.shape, jnp.int32),
+            pltpu.SMEM(pair_cols.shape, jnp.int32),
+            pltpu.VMEM(pao_energy.shape, jnp.float32),
             pltpu.VMEM((ROW, HEAD + naux, dom), jnp.bfloat16),
             pltpu.VMEM((dom, naux), jnp.bfloat16),
             pltpu.VMEM((naux, dom), jnp.float32),
@@ -430,11 +440,11 @@
             dma((ROW,)),
             dma((n_oi,)),
             dma((n_oi,)),
-            dma((5,)),
+            dma((8,)),
             pltpu.SemaphoreType.REGULAR((3,)),
         ],
         compiler_params=pltpu.CompilerParams(
-            collective_id=0, has_side_effects=True, vmem_limit_bytes=56 * 2**20
+            collective_id=0, has_side_effects=True, vmem_limit_bytes=52 * 2**20
         ),
         cost_estimate=pl.CostEstimate(
             flops=2 * naux * dom * dom * 32, bytes_accessed=4 * naux * dom, transcendentals=0

time: 134 us -> 133 us (level)
    pallas_call x1, Pallas kernels: 129 us -> 128 us  [body(): pl.pallas_call(functools.partial(kernel, n_oi), out_shape=(jax.ShapeDtype...]
    unnamed x4 -> x8, local copies, waits for them, and re-layouts: 3.29 us -> 3.83 us
where the time goes in v5:
time: 133 us
  Pallas kernels  128 us (96%)
  local copies, waits for them, and re-layouts  3.83 us (3%)
    pallas_call x1, Pallas kernels, body(): pl.pallas_call(functools.partial(kernel, n_oi), out_shape=(jax.ShapeDtype...  128 us
    unnamed x8, local copies, waits for them, and re-layouts  3.83 us

profile of v5, /device:TPU:1, one launch (start us, length us, event | category | flops | bytes accessed | tf_op | source)
XLA Modules:
  0.0 132.8 jit_solution(5947197344582748878)
XLA Ops:
  1.3 0.0 copy-start
  1.3 0.7 copy-done
  2.0 0.0 copy-start.1
  2.0 0.7 copy-done.1
  2.7 0.0 copy-start.2
  2.7 0.7 copy-done.2
  3.4 127.6 %shard_map.68 = (bf16[1,1536,512]{2,1,0:T(8,128)(2,1)S(1)}, bf16[12,1536]{1,0:T(8,128)(2,1)S(1)}) custom-call(bf16[1,1536,512]{2,1,0:T(8,128)(2,1)} %b_hbm.1, bf16[1,1]{1,0:T(2,128)(2,1)} %bitcast.1.occ_ref, s32[1,4]{1,0:T(1,128)S(1)} %copy-done.1, s32[1,7]{1,0:T(1,128)S(1)} %copy-done.2, f32[64,128]{1,0:T(8,128)S(1)} %copy-done), custom_call_target="tpu_custom_call" | custom-call | flops 25769803776 | bytes 3145728 | tf_op jit(solution)/shard_map/pallas_call | solution.py:415
  131.0 1.1 copy.10
  132.1 0.6 copy.11
Async XLA Ops:
  1.3 0.8 copy-start
  2.0 0.7 copy-start.1
  2.7 0.7 copy-start.2

commit v6 on v5

--- a/solution.py
+++ b/solution.py
@@ -315,7 +315,7 @@
 
     dacc[...] = jnp.zeros_like(dacc)
 
-    def density(i, carry):
+    def slices_in(i):
         for n in range(2):
             chip = pick(2 * i + n, ring)
             for k in range(CORES):
@@ -329,32 +329,30 @@
                 def _():
                     gamma_copy(source, source, source).wait_recv()
 
+    def four_terms(i, start=0, size=naux):
         terms = [
-            dot_nt(gall[pick(2 * i + n, ring) * CORES + k], block(pick(2 * i + n, ring) * CORES + k))
-            for n in range(2) for k in range(CORES)
+            dot_nt(gall[source], block(source, start, size))
+            for source in (pick(2 * i + n, ring) * CORES + k for n in range(2) for k in range(CORES))
         ]
-        dacc[...] += (terms[0] + terms[1]) + (terms[2] + terms[3])
+        return (terms[0] + terms[1]) + (terms[2] + terms[3])
+
+    def density(i, carry):
+        slices_in(i)
+        dacc[...] += four_terms(i)
         return carry
 
     lax.fori_loop(0, 1, density, 0)
     hear(1)
     tell(2)
-    lax.fori_loop(1, ROW // CORES // 2, density, 0)
+    lax.fori_loop(1, ROW // CORES // 2 - 1, density, 0)
     hear(2)
-    groups = 4
-    lanes = naux // groups
-    for t in range(n_oi):
-        rows = dacc[t * strip:(t + 1) * strip, :]
-        dpart[t] = jnp.concatenate(
-            [rows[:, g * lanes:(g + 1) * lanes] for g in range(groups)], axis=0
-        ).astype(jnp.bfloat16)
-
-    def den_copy(t, row, where):
+
+    def den_copy(t, row, where, third):
         return pltpu.make_async_remote_copy(
-            src_ref=dpart.at[t],
-            dst_ref=dall.at[row],
-            send_sem=den_send.at[t],
-            recv_sem=den_recv.at[row],
+            src_ref=dpart.at[t, third],
+            dst_ref=dall.at[row, third],
+            send_sem=den_send.at[t, third],
+            recv_sem=den_recv.at[row, third],
             device_id=where,
             device_id_type=MESH,
         )
@@ -364,10 +362,23 @@
     def keep_copy():
         return pltpu.make_async_copy(dpart.at[jnp.clip(own_strip, 0, n_oi - 1)], dall.at[oi], local_sem.at[2])
 
-    for t in range(n_oi):
-        @pl.when(first_owner + t != me)
-        def _():
-            den_copy(t, oi, owner(t)).start()
+    groups = 4
+    final = ROW // CORES // 2 - 1
+    wide = naux // 3
+    lanes = wide // groups
+    slices_in(final)
+    for third in range(3):
+        columns = slice(third * wide, (third + 1) * wide)
+        done = dacc[:, columns] + four_terms(final, third * wide, wide)
+        for t in range(n_oi):
+            rows = done[t * strip:(t + 1) * strip, :]
+            dpart[t, third] = jnp.concatenate(
+                [rows[:, g * lanes:(g + 1) * lanes] for g in range(groups)], axis=0
+            ).astype(jnp.bfloat16)
+        for t in range(n_oi):
+            @pl.when(first_owner + t != me)
+            def _():
+                den_copy(t, oi, owner(t), third).start()
 
     @pl.when(self_owner)
     def _():
@@ -390,19 +401,21 @@
     for row in range(n_oi):
         @pl.when(jnp.logical_or(oi != row, oj != my_slice))
         def _():
-            den_copy(0, row, (row, my_slice)).wait_recv()
+            for third in range(3):
+                den_copy(0, row, (row, my_slice), third).wait_recv()
     total = dall[0].astype(jnp.float32)
     for row in range(1, n_oi):
         total = total + dall[row].astype(jnp.float32)
     total = total * (1.0 / (n_oi * ROW))
     dens_out[...] = jnp.concatenate(
-        [total[g * strip:(g + 1) * strip] for g in range(groups)], axis=1
+        [total[third, g * strip:(g + 1) * strip] for third in range(3) for g in range(groups)], axis=1
     ).astype(jnp.bfloat16)
 
     for t in range(n_oi):
         @pl.when(first_owner + t != me)
         def _():
-            den_copy(t, oi, owner(t)).wait_send()
+            for third in range(3):
+                den_copy(t, oi, owner(t), third).wait_send()
 
 
 def body(n_oi, b_tensor, occ_energy, dom_blocks, pair_cols, pao_energy):
@@ -431,15 +444,15 @@
             pltpu.VMEM((ROW, slice_rows, dom), jnp.bfloat16),
             pltpu.VMEM((dom, CORES * dom), jnp.bfloat16),
             pltpu.VMEM((slice_rows, naux), jnp.float32),
-            pltpu.VMEM((n_oi, 4 * strip, naux // 4), jnp.bfloat16),
-            pltpu.VMEM((n_oi, 4 * strip, naux // 4), jnp.bfloat16),
+            pltpu.VMEM((n_oi, 3, 4 * strip, naux // 12), jnp.bfloat16),
+            pltpu.VMEM((n_oi, 3, 4 * strip, naux // 12), jnp.bfloat16),
             pltpu.VMEM((dom, 128), jnp.float32),
             dma((4, 24)),
             dma((ROW, 3)),
             dma((ROW,)),
             dma((ROW,)),
-            dma((n_oi,)),
-            dma((n_oi,)),
+            dma((n_oi, 3)),
+            dma((n_oi, 3)),
             dma((8,)),
             pltpu.SemaphoreType.REGULAR((3,)),
         ],

time: 133 us -> 132 us (level)
  no operation moved by 1% of the time
where the time goes in v6:
time: 132 us
  Pallas kernels  127 us (96%)
  local copies, waits for them, and re-layouts  3.83 us (3%)
    pallas_call x1, Pallas kernels, body(): pl.pallas_call(functools.partial(kernel, n_oi), out_shape=(jax.ShapeDtype...  127 us
    unnamed x8, local copies, waits for them, and re-layouts  3.83 us

profile of v6, /device:TPU:1, one launch (start us, length us, event | category | flops | bytes accessed | tf_op | source)
XLA Modules:
  0.0 132.2 jit_solution(5137365604994546567)
XLA Ops:
  1.3 0.0 copy-start
  1.3 0.7 copy-done
  2.0 0.0 copy-start.1
  2.0 0.7 copy-done.1
  2.7 0.0 copy-start.2
  2.7 0.7 copy-done.2
  3.4 127.1 %shard_map.68 = (bf16[1,1536,512]{2,1,0:T(8,128)(2,1)S(1)}, bf16[12,1536]{1,0:T(8,128)(2,1)S(1)}) custom-call(bf16[1,1536,512]{2,1,0:T(8,128)(2,1)} %b_hbm.1, bf16[1,1]{1,0:T(2,128)(2,1)} %bitcast.1.occ_ref, s32[1,4]{1,0:T(1,128)S(1)} %copy-done.1, s32[1,7]{1,0:T(1,128)S(1)} %copy-done.2, f32[64,128]{1,0:T(8,128)S(1)} %copy-done), custom_call_target="tpu_custom_call" | custom-call | flops 25769803776 | bytes 3145728 | tf_op jit(solution)/shard_map/pallas_call | solution.py:428
  130.4 1.1 copy.10
  131.6 0.6 copy.11
Async XLA Ops:
  1.3 0.8 copy-start
  2.0 0.7 copy-start.1
  2.7 0.7 copy-start.2
